TPU v7x, 32 devices: a whole 2x2x4 slice. The times are simulated.
32 devices in a mesh: tm: 8 (over y, x, core), space: 4 (over z).
Axes of the slice: x: 2, y: 2, z: 4, core: 2. Of those that a mesh axis runs over, the one named last changes fastest.
Arguments:
- start: float32 [8, 2, 32, 64, 128], P('tm', None, 'space'), may hold values from -0.2 to 1.2
- conduct: float32 [32, 64, 128], P('space'), may hold values from 0.03 to 0.12
- threshold: float32 [32, 64, 128], P('space'), may hold values from 0.05 to 0.45
- recovery: float32 [32, 64, 128], P('space'), may hold values from 0.02 to 0.3
Outputs:
- final: float32 [8, 2, 32, 64, 128], P('tm', None, 'space')
All inputs are finite; a program needn't handle non-finite values.
Results may differ from a plain program's by a relative error of at most 0.0001.
Values sent between devices are 32-bit elements; how exact they have to be, the bound alone decides.
A program may use at most 64 MiB of HBM per device.

v0:
```python
import functools
import jax
import jax.numpy as jnp
from jax import lax
from jax.experimental import pallas as pl
from jax.experimental.pallas import tpu as pltpu
from jax.sharding import PartitionSpec as P

MESH = pl.DeviceIdType.MESH
SIXTH = 1.0 / 6.0
W24 = 1.0 / 24.0


def react(e, t):
    return 2.0 * e * (1.0 - e) * (e - t)


def near(v, axis, by):
    if axis == 0:
        rows, lanes = v.shape
        groups = v.reshape(rows // 8, 8, lanes)
        at = lax.broadcasted_iota(jnp.int32, groups.shape, 1)
        none = jnp.zeros((1, 8, lanes), v.dtype)
        low = pltpu.roll(groups, by, 1)
        low = jnp.where(at < by, jnp.concatenate([none, low[:-1]], axis=0), low)
        high = pltpu.roll(groups, 8 - by, 1)
        high = jnp.where(at >= 8 - by, jnp.concatenate([high[1:], none], axis=0), high)
        return (low + high).reshape(rows, lanes)
    n = v.shape[axis]
    at = lax.broadcasted_iota(jnp.int32, v.shape, axis)
    low = jnp.where(at < by, 0.0, pltpu.roll(v, by, axis))
    high = jnp.where(at >= n - by, 0.0, pltpu.roll(v, n - by, axis))
    return low + high


def tiles(v, by):
    rows, lanes = v.shape
    return pltpu.roll(v.reshape(rows // 8, 8, lanes), by, 1).reshape(rows, lanes)


def even_rows(v):
    return lax.broadcasted_iota(jnp.int32, v.shape, 0) % 2 == 0


def pair(v):
    return v + jnp.where(even_rows(v), tiles(v, 7), tiles(v, 1))


def fold(v):
    half = v.shape[0] // 2
    return jnp.where(even_rows(v[:half]), v[:half], v[half:])


def expand(x):
    even = even_rows(x)
    return jnp.where(even, x, tiles(x, 1)), jnp.where(even, tiles(x, 7), x)


def unfold(x):
    return jnp.concatenate(expand(x), axis=0)


def inplane(e):
    return near(e, 0, 1) + near(e, 1, 1) - 6.0 * e


MESSAGES = {
    name: at
    for at, name in enumerate(
        [
            (kind, side)
            for kind in ("q", "c", "n1p", "n2", "dp", "n2x", "j", "jx", "m1", "m2p", "d2")
            for side in (0, 1)
        ]
        + [(kind, side) for kind in ("n2r", "n2e", "jt") for side in (0, 1, 2)]
    )
}


def kernel(
    start, cond, thr, rec, node_out, jump_out,
    qe, qr, c, t, k, cc, tc, kc,
    f0e, f0r, n1e, n1r, n2e, n2r, t1e, t1r,
    dE, dR, jE, jR, u1e, u2e, s1e, s1r, s2e, s2r,
    qne, qnr, m1e, m1r, m2e, m2r, t0e, t0r,
    n1s, n1h, ds, dh, js, jh, jxh, n2xh, rn2r, rn2e, jts, jth,
    m2s, m2h, d2s, d2h,
    load_sem, store_sem, send_sem, recv_sem,
):
    nx = qr.shape[0]
    cn = nx // 2
    p, s = lax.axis_index("tm"), lax.axis_index("space")
    slices, slabs = lax.axis_size("tm"), lax.axis_size("space")
    head = p == 0
    has = (s > 0, s < slabs - 1)
    earlier, later = p > 0, p < slices - 1
    plane = qe.shape[1:]
    zeros = jnp.zeros(plane, jnp.float32)

    loads = [
        pltpu.make_async_copy(src, dst, load_sem.at[i])
        for i, (src, dst) in enumerate(
            [
                (start.at[0, 0], qe.at[pl.ds(1, nx)]),
                (cond, c.at[pl.ds(1, nx)]),
                (thr, t),
                (start.at[0, 1], qr),
                (rec, k),
            ]
        )
    ]
    for load in loads:
        load.start()

    barrier = pltpu.get_barrier_semaphore()

    def greet(when, dp, dside):
        @pl.when(when)
        def _():
            pl.semaphore_signal(barrier, inc=1, device_id=(p + dp, s + dside), device_id_type=MESH)

    greet(has[0], 0, -1)
    greet(has[1], 0, 1)
    greet(earlier, -1, 0)
    greet(earlier & has[0], -1, -1)
    greet(earlier & has[1], -1, 1)

    for side in (0, 1):
        end = side * (nx + 1)

        @pl.when(jnp.logical_not(has[side]))
        def _():
            for ref in (qe, c):
                ref[end] = zeros
            for ref in (n1h, n2xh, m2h):
                ref[side] = zeros
            n2e[end] = zeros
            m1e[end] = zeros
            for ref in (dh, jh, jxh, d2h):
                ref[side] = zeros[: plane[0] // 2]

    sides = has[0].astype(jnp.int32) + has[1].astype(jnp.int32)
    after = later.astype(jnp.int32)
    pl.semaphore_wait(barrier, sides + after * (sides + 1))

    pending = []

    def copy_of(name, src, dst, dp, dside):
        at = MESSAGES[name]
        return pltpu.make_async_remote_copy(
            src_ref=src,
            dst_ref=dst,
            send_sem=send_sem.at[at],
            recv_sem=recv_sem.at[at],
            device_id=(p + dp, s + dside),
            device_id_type=MESH,
        )

    def send(name, src, dst, when, dp=0, dside=0):
        @pl.when(when)
        def _():
            copy_of(name, src, dst, dp, dside).start()

        pending.append((name, src, dst, when, dp, dside))

    def receive(name, dst, when):
        @pl.when(when)
        def _():
            copy_of(name, dst, dst, 0, 0).wait_recv()

    def to_sides(kind, src, dst):
        for side in (0, 1):
            send((kind, side), src(side), dst(1 - side), has[side], 0, 2 * side - 1)

    def to_later_sides(kind, src, dst):
        for side in (0, 1):
            send((kind, side), src(side), dst(1 - side), later & has[side], 1, 2 * side - 1)

    def from_side(kind, side, dst, when=None):
        receive((kind, 1 - side), dst, has[side] if when is None else when & has[side])

    def edge(side):
        return side * (nx - 1)

    def halo(ref):
        return lambda side: ref.at[side * (ref.shape[0] - 1)]

    def slot(ref):
        return lambda side: ref.at[side]

    def each(low, high, body):
        def step(i, _):
            body(i)
            return 0

        lax.fori_loop(low, high, step, 0)

    def on_edges(body):
        each(0, 2, lambda side: body(side, side * (nx - 1), 2 + side * (nx - 3)))

    to_sides("q", lambda side: start.at[0, 0, edge(side)], halo(qe))
    to_sides("c", lambda side: cond.at[edge(side)], halo(c))
    for load in loads:
        load.wait()

    def first_edge(side, i, inner):
        e, r = qe[i + 1], qr[i]
        f = c[i + 1] * (qe[inner] + inplane(e)) + react(e, t[i]) - r
        g = k[i] * (e - 0.5 * r)
        f0e[i], f0r[i] = f, g
        n1 = e + 0.5 * f
        n1e[i + 1], n1s[side], n1r[i] = n1, n1, r + 0.5 * g

    on_edges(first_edge)
    to_sides("n1p", slot(n1s), slot(n1h))

    def slow_step(i):
        g = k[i] * (n1e[i + 1] - 0.5 * n1r[i])
        t1r[i] = g
        n2r[i] = n1r[i] + 0.5 * g

    def first_inner(i):
        e, r = qe[i + 1], qr[i]
        f = c[i + 1] * (qe[i] + qe[i + 2] + inplane(e)) + react(e, t[i]) - r
        g = k[i] * (e - 0.5 * r)
        f0e[i], f0r[i] = f, g
        n1e[i + 1], n1r[i] = e + 0.5 * f, r + 0.5 * g
        slow_step(i)

    each(1, nx - 1, first_inner)

    def hand_over(kind, part, ref, shift, dst, low, count):
        src = ref.at[pl.ds(low + shift, count)]
        send((kind, part), src, dst.at[pl.ds(low, count)], later, 1)

    hand_over("n2r", 2, n2r, 0, rn2r, 1, nx - 2)

    def second(i):
        e = n1e[i + 1]
        f = c[i + 1] * (n1e[i] + n1e[i + 2] + inplane(e)) + react(e, t[i]) - n1r[i]
        t1e[i] = f
        n2e[i + 1] = e + 0.5 * f

    each(2, nx - 2, second)
    hand_over("n2e", 2, n2e, 1, rn2e, 2, nx - 4)

    def coarse_coeffs(j):
        for fine, shift, coarse in ((c, 1, cc), (t, 0, tc), (k, 0, kc)):
            coarse[j] = 0.25 * pair(fine[2 * j + shift] + fine[2 * j + 1 + shift])

    each(0, cn, coarse_coeffs)

    for side in (0, 1):
        i, end = edge(side), side * (nx + 1)
        from_side("q", side, qe.at[end])
        from_side("c", side, c.at[end])
        from_side("n1p", side, n1h.at[side])
        more = c[i + 1] * qe[end]
        f0e[i] += more
        n1e[i + 1] += 0.5 * more
        n1e[end] = n1h[side] + 0.5 * c[end] * qe[i + 1]
        slow_step(i)

    on_edges(lambda side, i, inner: second(i))
    own_edge = lambda ref: lambda side: ref.at[edge(side) + 1]
    to_sides("n2", own_edge(n2e), halo(n2e))
    on_edges(lambda side, i, inner: second(inner - 1))
    for side in (0, 1):
        hand_over("n2e", side, n2e, 1, rn2e, side * (nx - 2), 2)
        hand_over("n2r", side, n2r, 0, rn2r, edge(side), 1)

    def third(j, e_ref, r_ref, extra, missing=None):
        sums = [0.0, 0.0, 0.0, 0.0]
        for row in (0, 1):
            i = 2 * j + row
            e, r = e_ref[i + 1], r_ref[i]
            if missing == 0 and row == 0:
                x = e_ref[i + 2]
            elif missing == 1 and row == 1:
                x = e_ref[i]
            else:
                x = e_ref[i] + e_ref[i + 2]
            fe = c[i + 1] * (x + inplane(e)) + react(e, t[i]) - r
            fr = k[i] * (e - 0.5 * r)
            a, b, g, h = extra(i)
            sums[0] += a - W24 * fe
            sums[1] += b - W24 * fr
            sums[2] += g + SIXTH * fe
            sums[3] += h + SIXTH * fr
        dE[j + 1] = 0.25 * pair(sums[0])
        dR[j] = 0.25 * pair(sums[1])
        jE[j] = 0.25 * pair(sums[2])
        jR[j] = 0.25 * pair(sums[3])

    def extra_first(i):
        a, b, g, h = f0e[i], t1e[i], f0r[i], t1r[i]
        return (
            8 * W24 * b - 7 * W24 * a,
            8 * W24 * h - 7 * W24 * g,
            SIXTH * b - 2 * SIXTH * a,
            SIXTH * h - 2 * SIXTH * g,
        )

    for side in (0, 1):
        third(side * (cn - 1), n2e, n2r, extra_first, side)
        ds[side] = fold(dE[side * (cn - 1) + 1])
    to_sides("dp", slot(ds), slot(dh))
    to_later_sides("n2x", own_edge(n2e), slot(n2xh))
    each(1, cn - 1, lambda j: third(j, n2e, n2r, extra_first))

    def coarse_step(j, node, x):
        d, dr = dE[j + 1], dR[j]
        lap = 0.25 * (x + near(d, 0, 2)) + near(d, 1, 1) - 3.0 * d
        b = 0.25 * pair(node[2 * j + 1] + node[2 * j + 2])
        return 0.5 * (cc[j] * lap + react(b + d, tc[j]) - react(b, tc[j]) - dr)

    def coarse_slow(j):
        return jR[j] + 0.5 * kc[j] * (dE[j + 1] - 0.5 * dR[j])

    def coarse_first(j):
        e = jE[j] + coarse_step(j, n1e, dE[j] + dE[j + 2])
        r = coarse_slow(j)
        jE[j], jR[j] = e, r
        jts[j] = jnp.where(even_rows(e), e, r)

    each(1, cn - 1, coarse_first)
    send(("jt", 2), jts.at[pl.ds(1, cn - 2)], jth.at[pl.ds(1, cn - 2)], later, 1)

    for side in (0, 1):
        i, j, end = edge(side), side * (cn - 1), side * (nx + 1)
        from_side("n2", side, n2e.at[end])
        from_side("dp", side, dh.at[side])
        more = 0.25 * pair(c[i + 1] * n2e[end])
        change = W24 * more
        dE[j + 1] -= change
        beside = 1 + side * (cn - 3)
        jE[beside] -= 0.125 * cc[beside] * change
        jE[j] += SIXTH * more
        dE[side * (cn + 1)] = unfold(dh[side]) - (0.25 * W24) * pair(c[end] * n2e[i + 1])

    each(0, 2, lambda side: coarse_first(side * (cn - 1)))
    for side in (0, 1):
        js[side] = fold(jE[side * (cn - 1)])
    to_sides("j", slot(js), slot(jh))
    to_later_sides("jx", slot(js), slot(jxh))
    for side in (0, 1):
        last = pl.ds(side * (cn - 1), 1)
        send(("jt", side), jts.at[last], jth.at[last], later, 1)

    def correct(j):
        for row in (0, 1):
            i = 2 * j + row
            u1e[i + 1] = n1e[i + 1] + dE[j + 1]
            u2e[i + 1] = n2e[i + 1] + jE[j]

    each(0, cn, correct)
    for side in (0, 1):
        end = side * (nx + 1)
        u1e[end] = n1e[end] + dE[side * (cn + 1)]
        u2e[end] = zeros

    def old_terms(j):
        for row in (0, 1):
            i = 2 * j + row
            u1, u2 = u1e[i + 1], u2e[i + 1]
            u1r, u2r = n1r[i] + dR[j], n2r[i] + jR[j]
            a1 = c[i + 1] * (u1e[i] + u1e[i + 2] + inplane(u1)) + react(u1, t[i]) - u1r
            a2 = c[i + 1] * (u2e[i] + u2e[i + 2] + inplane(u2)) + react(u2, t[i]) - u2r
            b1 = k[i] * (u1 - 0.5 * u1r)
            b2 = k[i] * (u2 - 0.5 * u2r)
            a0, b0 = f0e[i], f0r[i]
            s1e[i] = 8 * W24 * a1 - 7 * W24 * a0 - W24 * a2
            s1r[i] = 8 * W24 * b1 - 7 * W24 * b0 - W24 * b2
            s2e[i] = 5 * W24 * a2 - W24 * a0 - 4 * W24 * a1
            s2r[i] = 5 * W24 * b2 - W24 * b0 - 4 * W24 * b1

    each(0, cn, old_terms)

    for side in (0, 1):
        i, end = edge(side), side * (nx + 1)
        from_side("j", side, jh.at[side])
        more = c[i + 1] * (n2e[end] + unfold(jh[side]))
        s1e[i] -= W24 * more
        s2e[i] += 5 * W24 * more

    receive(("n2r", 2), rn2r.at[pl.ds(1, nx - 2)], earlier)
    receive(("n2e", 2), rn2e.at[pl.ds(2, nx - 4)], earlier)
    for side in (0, 1):
        receive(("n2r", side), rn2r.at[pl.ds(edge(side), 1)], earlier)
        receive(("n2e", side), rn2e.at[pl.ds(side * (nx - 2), 2)], earlier)
    for side in (0, 1):
        from_side("n2x", side, n2xh.at[side], earlier)
        from_side("jx", side, jxh.at[side], earlier)
        end = side * (nx + 1)
        qne[end] = jnp.where(head, qe[end], n2xh[side] + unfold(jxh[side]))
    receive(("jt", 2), jth.at[pl.ds(1, cn - 2)], earlier)
    for side in (0, 1):
        receive(("jt", side), jth.at[pl.ds(side * (cn - 1), 1)], earlier)

    def arrive(j, side=None):
        e, r = expand(jth[j])
        if side is not None:
            e -= (0.125 * W24 * 0.25) * cc[j] * pair(c[edge(side) + 1] * n2xh[side])
        for row in (0, 1):
            i = 2 * j + row
            qne[i + 1] = jnp.where(head, qe[i + 1], rn2e[i] + e)
            qnr[i] = jnp.where(head, qr[i], rn2r[i] + r)

    each(0, 2, lambda side: arrive(side * (cn - 1)))
    for side in (0, 1):
        arrive(1 + side * (cn - 3), side)
    each(2, cn - 2, arrive)

    def next_first(i):
        e, r = qne[i + 1], qnr[i]
        f = c[i + 1] * (qne[i] + qne[i + 2] + inplane(e)) + react(e, t[i]) - r
        g = k[i] * (e - 0.5 * r)
        t0e[i], t0r[i] = f, g
        m1e[i + 1] = e + 0.5 * f + s1e[i]
        m1r[i] = r + 0.5 * g + s1r[i]

    on_edges(lambda side, i, inner: next_first(i))
    to_sides("m1", own_edge(m1e), halo(m1e))
    on_edges(lambda side, i, inner: next_first(inner - 1))

    def next_second(i, x):
        e, r = m1e[i + 1], m1r[i]
        f = c[i + 1] * (x + inplane(e)) + react(e, t[i]) - r
        g = k[i] * (e - 0.5 * r)
        t1e[i], t1r[i] = f, g
        m2 = e + 0.5 * f + s2e[i]
        m2e[i + 1] = m2
        m2r[i] = r + 0.5 * g + s2r[i]
        return m2

    def next_edge(side, i, inner):
        m2s[side] = next_second(i, m1e[inner])

    on_edges(next_edge)
    to_sides("m2p", slot(m2s), slot(m2h))
    each(2, nx - 2, next_first)
    each(1, nx - 1, lambda i: next_second(i, m1e[i] + m1e[i + 2]))

    for side in (0, 1):
        i, end = edge(side), side * (nx + 1)
        from_side("m1", side, m1e.at[end])
        from_side("m2p", side, m2h.at[side])
        more = c[i + 1] * m1e[end]
        t1e[i] += more
        m2e[i + 1] += 0.5 * more
        m2e[end] = m2h[side] + 0.5 * c[end] * m1e[i + 1]

    stores = []

    def store(src, dst):
        stores.append(pltpu.make_async_copy(src, dst, store_sem.at[len(stores)]))
        stores[-1].start()

    store(m2e.at[pl.ds(1, nx)], node_out.at[0])
    store(m2r, node_out.at[1])

    def extra_next(i):
        a, b, g, h = t0e[i], t1e[i], t0r[i], t1r[i]
        return (
            8 * W24 * b - 7 * W24 * a - s1e[i],
            8 * W24 * h - 7 * W24 * g - s1r[i],
            SIXTH * b - 2 * SIXTH * a - s1e[i] - s2e[i],
            SIXTH * h - 2 * SIXTH * g - s1r[i] - s2r[i],
        )

    each(0, 2, lambda side: third(side * (cn - 1), m2e, m2r, extra_next))
    for side in (0, 1):
        d2s[side] = fold(dE[side * (cn - 1) + 1])
    to_sides("d2", slot(d2s), slot(d2h))
    each(1, cn - 1, lambda j: third(j, m2e, m2r, extra_next))

    def final_slow(j):
        jR[j] = coarse_slow(j)

    each(0, cn, final_slow)
    store(jR, jump_out.at[1])

    def final_fast(j):
        jE[j] += coarse_step(j, m1e, dE[j] + dE[j + 2])

    each(1, cn - 1, final_fast)
    inside = pl.ds(1, cn - 2)
    store(jE.at[inside], jump_out.at[0, inside])

    for side in (0, 1):
        j = side * (cn - 1)
        jE[j] += coarse_step(j, m1e, dE[2 + side * (cn - 3)])
    for side in (0, 1):
        j = side * (cn - 1)
        from_side("d2", side, d2h.at[side])
        jE[j] += 0.125 * cc[j] * unfold(d2h[side])
        store(jE.at[j], jump_out.at[0, j])

    for name, src, dst, when, dp, dside in pending:

        @pl.when(when)
        def _():
            copy_of(name, src, dst, dp, dside).wait_send()

    for stored in stores:
        stored.wait()


def per_device(start, conduct, threshold, recovery):
    nx, ny, nz = conduct.shape
    cn = nx // 2

    def planes(count, rows=ny):
        return pltpu.VMEM((count, rows, nz), jnp.float32)

    own, padded, coarse, two, half = (
        planes(nx), planes(nx + 2), planes(cn), planes(2), planes(2, ny // 2)
    )
    scratch = [
        padded, own, padded, own, own, coarse, coarse, coarse,
        own, own, padded, own, padded, own, own, own,
        planes(cn + 2), coarse, coarse, coarse, padded, padded, own, own, own, own,
        padded, own, padded, own, padded, own, own, own,
        two, two, half, half, half, half, half, two, own, own, coarse, coarse,
        two, two, half, half,
        pltpu.SemaphoreType.DMA((5,)),
        pltpu.SemaphoreType.DMA((6,)),
        pltpu.SemaphoreType.DMA((len(MESSAGES),)),
        pltpu.SemaphoreType.DMA((len(MESSAGES),)),
    ]
    nodes, jumps = pl.pallas_call(
        kernel,
        out_shape=[
            jax.ShapeDtypeStruct((2, nx, ny, nz), jnp.float32),
            jax.ShapeDtypeStruct((2, cn, ny, nz), jnp.float32),
        ],
        in_specs=[pl.BlockSpec(memory_space=pl.ANY)] * 4,
        out_specs=[pl.BlockSpec(memory_space=pl.ANY)] * 2,
        scratch_shapes=scratch,
        compiler_params=pltpu.CompilerParams(
            collective_id=0, has_side_effects=True, vmem_limit_bytes=62 * 1024 * 1024
        ),
    )(start, conduct, threshold, recovery)
    corrected = nodes.reshape(2, cn, 2, ny, nz) + jumps[:, :, None]
    return corrected.reshape(start.shape)


def solution(mesh):
    placed = (
        P("tm", None, "space", None, None),
        P("space", None, None),
        P("space", None, None),
        P("space", None, None),
    )
    return jax.shard_map(
        per_device,
        mesh=mesh,
        in_specs=placed,
        out_specs=P("tm", None, "space", None, None),
        check_vma=False,
    )
```

profile of v0, /device:TPU:0, one launch (start us, length us, event | category | flops | bytes accessed | tf_op | source)
XLA Modules:
  0.0 24.9 jit_solution(14461389010080647900)
XLA Ops:
  0.0 22.9 %shard_map.46 = (f32[2,8,64,128]{3,2,1,0:T(8,128)}, f32[2,4,64,128]{3,2,1,0:T(8,128)}) custom-call(f32[1,2,8,64,128]{4,3,2,1,0:T(8,128)} %start.1, f32[8,64,128]{2,1,0:T(8,128)} %cond.1, f32[8,64,128]{2,1,0:T(8,128)} %thr.1, f32[8,64,128]{2,1,0:T(8,128)} %rec.1), custom_call_target="tpu_custom_call" | custom-call | tf_op jit(solution)/shard_map/pallas_call | solution.py:531
  23.0 0.0 copy-start
  23.0 1.1 %add.14 = f32[2,4,2,64,128]{4,3,2,1,0:T(8,128)S(1)} broadcast(f32[2,4,64,128]{3,2,1,0:T(8,128)} %get-tuple-element.8), dimensions={0,1,3,4} | broadcast | bytes 786432 | tf_op jit(solution)/shard_map/add | solution.py:544
  24.0 0.1 copy-done
  24.1 0.9 %add_bitcast_fusion = f32[1,2,8,64,128]{4,3,2,1,0:T(8,128)} fusion(f32[2,8,64,128]{3,2,1,0:T(8,128)S(1)} %copy-done, f32[2,8,64,128]{3,2,1,0:T(8,128)S(1)} %bitcast.3), kind=kLoop, calls=%fused_computation | loop fusion | flops 131072 | bytes 1572864 | tf_op jit(solution)/shard_map/add | solution.py:544
Async XLA Ops:
  23.0 1.1 %copy-start = (f32[2,8,64,128]{3,2,1,0:T(8,128)S(1)}, f32[2,8,64,128]{3,2,1,0:T(8,128)}, u32[]{:S(2)}) copy-start(f32[2,8,64,128]{3,2,1,0:T(8,128)} %get-tuple-element.7) | copy-start | bytes 1572868
where the time goes:
time: 25.1 us; the launch traced here: 24.9 us
  Pallas kernels  22.9 us (91%)
  local copies, waits for them, and re-layouts  1.11 us (4%)
  other arithmetic  0.86 us (3%)
    pallas_call x1, Pallas kernels, per_device(): pl.pallas_call(kernel, out_shape=[jax.ShapeDtypeStruct((2, nx, ny, nz), j...  22.9 us
    add x1, local copies, waits for them, and re-layouts, per_device(): corrected = nodes.reshape(2, cn, 2, ny, nz) + jumps[:, :, None]  1.05 us
    add x1, other arithmetic, per_device(): corrected = nodes.reshape(2, cn, 2, ny, nz) + jumps[:, :, None]  0.86 us

commit v1 on v0

--- a/solution.py
+++ b/solution.py
@@ -69,7 +69,7 @@
     for at, name in enumerate(
         [
             (kind, side)
-            for kind in ("q", "c", "n1p", "n2", "dp", "n2x", "j", "jx", "m1", "m2p", "d2")
+            for kind in ("q", "c", "n1p", "n2", "dp", "n2x", "j", "jx", "m1", "m2p", "dw", "t1", "c2")
             for side in (0, 1)
         ]
         + [(kind, side) for kind in ("n2r", "n2e", "jt") for side in (0, 1, 2)]
@@ -84,7 +84,7 @@
     dE, dR, jE, jR, u1e, u2e, s1e, s1r, s2e, s2r,
     qne, qnr, m1e, m1r, m2e, m2r, t0e, t0r,
     n1s, n1h, ds, dh, js, jh, jxh, n2xh, rn2r, rn2e, jts, jth,
-    m2s, m2h, d2s, d2h,
+    m2s, m2h, dws, dwh, t1h, c2h,
     load_sem, store_sem, send_sem, recv_sem,
 ):
     nx = qr.shape[0]
@@ -132,11 +132,11 @@
         def _():
             for ref in (qe, c):
                 ref[end] = zeros
-            for ref in (n1h, n2xh, m2h):
+            for ref in (n1h, n2xh, m2h, t1h, c2h):
                 ref[side] = zeros
             n2e[end] = zeros
             m1e[end] = zeros
-            for ref in (dh, jh, jxh, d2h):
+            for ref in (dh, jh, jxh, dwh):
                 ref[side] = zeros[: plane[0] // 2]
 
     sides = has[0].astype(jnp.int32) + has[1].astype(jnp.int32)
@@ -347,6 +347,9 @@
         last = pl.ds(side * (cn - 1), 1)
         send(("jt", side), jts.at[last], jth.at[last], later, 1)
 
+    to_sides("t1", lambda side: thr.at[edge(side)], slot(t1h))
+    to_sides("c2", lambda side: cond.at[1 + side * (nx - 3)], slot(c2h))
+
     def correct(j):
         for row in (0, 1):
             i = 2 * j + row
@@ -441,6 +444,19 @@
     each(2, nx - 2, next_first)
     each(1, nx - 1, lambda i: next_second(i, m1e[i] + m1e[i + 2]))
 
+    def defect(i):
+        return 8 * W24 * t1e[i] - 7 * W24 * t0e[i] - s1e[i]
+
+    def next_defect(side, i, inner):
+        second, third_at = inner - 1, 2 + side * (nx - 5)
+        e = m2e[second + 1]
+        rest = c[second + 1] * (m2e[third_at + 1] + inplane(e)) + react(e, t[second])
+        rest = rest - m2r[second] - m2r[i] + c[i + 1] * e
+        dws[side] = fold(0.25 * pair(defect(i) + defect(second) - W24 * rest))
+
+    on_edges(next_defect)
+    to_sides("dw", slot(dws), slot(dwh))
+
     for side in (0, 1):
         i, end = edge(side), side * (nx + 1)
         from_side("m1", side, m1e.at[end])
@@ -468,33 +484,31 @@
             SIXTH * h - 2 * SIXTH * g - s1r[i] - s2r[i],
         )
 
-    each(0, 2, lambda side: third(side * (cn - 1), m2e, m2r, extra_next))
-    for side in (0, 1):
-        d2s[side] = fold(dE[side * (cn - 1) + 1])
-    to_sides("d2", slot(d2s), slot(d2h))
-    each(1, cn - 1, lambda j: third(j, m2e, m2r, extra_next))
+    each(0, cn, lambda j: third(j, m2e, m2r, extra_next))
 
     def final_slow(j):
         jR[j] = coarse_slow(j)
 
     each(0, cn, final_slow)
-    store(jR, jump_out.at[1])
+    for row in (0, 1):
+        store(jR, jump_out.at[1, :, row])
+
+    for side in (0, 1):
+        i, end = edge(side), side * (nx + 1)
+        from_side("dw", side, dwh.at[side])
+        from_side("t1", side, t1h.at[side])
+        from_side("c2", side, c2h.at[side])
+        own, beyond = m2e[i + 1], m2e[end]
+        rest = c[end] * (own + inplane(beyond)) + react(beyond, t1h[side]) + c2h[side] * beyond
+        more = 8 * W24 * c[end] * m1e[i + 1] - W24 * rest
+        dE[side * (cn + 1)] = unfold(dwh[side]) + 0.25 * pair(more)
 
     def final_fast(j):
         jE[j] += coarse_step(j, m1e, dE[j] + dE[j + 2])
 
-    each(1, cn - 1, final_fast)
-    inside = pl.ds(1, cn - 2)
-    store(jE.at[inside], jump_out.at[0, inside])
-
-    for side in (0, 1):
-        j = side * (cn - 1)
-        jE[j] += coarse_step(j, m1e, dE[2 + side * (cn - 3)])
-    for side in (0, 1):
-        j = side * (cn - 1)
-        from_side("d2", side, d2h.at[side])
-        jE[j] += 0.125 * cc[j] * unfold(d2h[side])
-        store(jE.at[j], jump_out.at[0, j])
+    each(0, cn, final_fast)
+    for row in (0, 1):
+        store(jE, jump_out.at[0, :, row])
 
     for name, src, dst, when, dp, dside in pending:
 
@@ -522,7 +536,7 @@
         planes(cn + 2), coarse, coarse, coarse, padded, padded, own, own, own, own,
         padded, own, padded, own, padded, own, own, own,
         two, two, half, half, half, half, half, two, own, own, coarse, coarse,
-        two, two, half, half,
+        two, two, half, half, two, two,
         pltpu.SemaphoreType.DMA((5,)),
         pltpu.SemaphoreType.DMA((6,)),
         pltpu.SemaphoreType.DMA((len(MESSAGES),)),
@@ -532,7 +546,7 @@
         kernel,
         out_shape=[
             jax.ShapeDtypeStruct((2, nx, ny, nz), jnp.float32),
-            jax.ShapeDtypeStruct((2, cn, ny, nz), jnp.float32),
+            jax.ShapeDtypeStruct((2, cn, 2, ny, nz), jnp.float32),
         ],
         in_specs=[pl.BlockSpec(memory_space=pl.ANY)] * 4,
         out_specs=[pl.BlockSpec(memory_space=pl.ANY)] * 2,
@@ -541,8 +555,7 @@
             collective_id=0, has_side_effects=True, vmem_limit_bytes=62 * 1024 * 1024
         ),
     )(start, conduct, threshold, recovery)
-    corrected = nodes.reshape(2, cn, 2, ny, nz) + jumps[:, :, None]
-    return corrected.reshape(start.shape)
+    return (nodes + jumps.reshape(2, nx, ny, nz)).reshape(start.shape)
 
 
 def solution(mesh):

time: 25.1 us -> 24.2 us (0.964)
  other arithmetic: 0.86 us -> 2.06 us
  local copies, waits for them, and re-layouts: 1.11 us -> 0 us
  Pallas kernels: 22.9 us -> 22 us
    reshape x0 -> x1, other arithmetic: none -> 2.06 us  [per_device(): return (nodes + jumps.reshape(2, nx, ny, nz)).reshape(start.shape)]
    add x1 -> x0, local copies, waits for them, and re-layouts: 1.05 us -> none  [per_device(): corrected = nodes.reshape(2, cn, 2, ny, nz) + jumps[:, :, None]]
    pallas_call x1, Pallas kernels: 22.9 us -> 22 us  [per_device(): pl.pallas_call(kernel, out_shape=[jax.ShapeDtypeStruct((2, nx, ny, nz), j...]
    add x1 -> x0, other arithmetic: 0.86 us -> none  [per_device(): corrected = nodes.reshape(2, cn, 2, ny, nz) + jumps[:, :, None]]
where the time goes in v1:
time: 24.2 us; the launch traced here: 24.1 us
  Pallas kernels  22 us (91%)
  other arithmetic  2.06 us (9%)
    pallas_call x1, Pallas kernels, per_device(): pl.pallas_call(kernel, out_shape=[jax.ShapeDtypeStruct((2, nx, ny, nz), j...  22 us
    reshape x1, other arithmetic, per_device(): return (nodes + jumps.reshape(2, nx, ny, nz)).reshape(start.shape)  2.06 us

profile of v1, /device:TPU:0, one launch (start us, length us, event | category | flops | bytes accessed | tf_op | source)
XLA Modules:
  0.0 24.1 jit_solution(13733058605015899942)
XLA Ops:
  0.0 22.0 %shard_map.46 = (f32[2,8,64,128]{3,2,1,0:T(8,128)}, f32[2,4,2,64,128]{4,3,2,1,0:T(8,128)}) custom-call(f32[1,2,8,64,128]{4,3,2,1,0:T(8,128)} %start.1, f32[8,64,128]{2,1,0:T(8,128)} %cond.1, f32[8,64,128]{2,1,0:T(8,128)} %thr.1, f32[8,64,128]{2,1,0:T(8,128)} %rec.1), custom_call_target="tpu_custom_call" | custom-call | tf_op jit(solution)/shard_map/pallas_call | solution.py:545
  22.0 2.1 %add_bitcast_fusion = f32[1,2,8,64,128]{4,3,2,1,0:T(8,128)} fusion(f32[2,8,64,128]{3,2,1,0:T(8,128)} %get-tuple-element.7, f32[2,8,64,128]{3,2,1,0:T(8,128)} %bitcast.3), kind=kLoop, calls=%fused_computation | loop fusion | flops 131072 | bytes 1572864 | tf_op jit(solution)/shard_map/reshape | solution.py:558
